TPU v7x, 32 devices: a whole 2x2x4 slice. The times are simulated.
32 devices in a mesh: query: 2 (over x), corpus: 16 (over z, y, core).
Axes of the slice: x: 2, y: 2, z: 4, core: 2. Of those that a mesh axis runs over, the one named last changes fastest.
Arguments:
- clean_feats: bfloat16 [2, 2, 512, 320], P('query', None, 'corpus'), may hold values from -6 to 6
- noise_draw: bfloat16 [2, 2, 512, 320], P('query', None, 'corpus'), may hold values from -6 to 6
- timesteps: int32 [2, 2], P('query'), may hold values from 0 to 999
- weight_in: bfloat16 [2, 320, 320], P(None, None, 'corpus'), may hold values from -0.3125 to 0.3125
- weight_ffin: bfloat16 [2, 320, 2560], P(None, None, 'corpus'), may hold values from -0.3125 to 0.3125
- weight_ffout: bfloat16 [2, 1280, 320], P(None, None, 'corpus'), may hold values from -0.15625 to 0.15625
- weight_out: bfloat16 [2, 320, 320], P(None, None, 'corpus'), may hold values from -0.3125 to 0.3125
- norm_gain: float32 [2, 320], replicated, may hold values from 0.5 to 1.5
- norm_bias: float32 [2, 320], replicated, may hold values from -3 to 3
- sketch_cin: bfloat16 [2, 3, 320, 16], replicated, may hold values from -0.3125 to 0.3125
- sketch_fin: bfloat16 [2, 1280, 16], replicated, may hold values from -0.15625 to 0.15625
- sketch_cout: bfloat16 [2, 3, 320, 16], replicated, may hold values from -0.3125 to 0.3125
- sketch_fout: bfloat16 [2, 2560, 16], replicated, may hold values from -0.125 to 0.125
- precond: float32 [8, 256, 256], P('query'), as said below
- store_grads: bfloat16 [8192, 2048], P(('query', 'corpus')), may hold values from -6 to 6
- store_scale: float32 [8192], P(('query', 'corpus')), may hold values from 0.002 to 0.03
Outputs:
- scores: float32 [2, 8192], P(None, ('query', 'corpus'))
Inputs may be any that keep to these rules, and one draw needn't show every extreme that they name: `precond`: each layer's matrix is symmetric with a diagonal between 1 and 2.
All inputs are finite; a program needn't handle non-finite values.
Results may differ from a plain program's by a relative error of at most 0.0085.
Values may be sent and summed in bfloat16 or wider, within the bound.
A program may use at most 64 MiB of HBM per device.

v0:
```python
import math
import jax
import jax.numpy as jnp
from jax import lax
from jax.sharding import PartitionSpec as P

plan_len = 1000


def noise_levels(timesteps):
    steps = jnp.arange(plan_len, dtype=jnp.float32)
    rooted = math.sqrt(0.00085) + (math.sqrt(0.012) - math.sqrt(0.00085)) * steps / (plan_len - 1)
    terms = jnp.log1p(-rooted * rooted)
    reached = jnp.arange(plan_len, dtype=jnp.int32) <= timesteps[..., None]
    picked = jnp.exp(jnp.sum(jnp.where(reached, terms, jnp.zeros_like(terms)), axis=-1))
    return (jnp.sqrt(picked), jnp.sqrt(1.0 - picked))


def gelu_parts(gate):
    cumul = 0.5 * (1.0 + jax.scipy.special.erf(gate / math.sqrt(2.0)))
    density = jnp.exp(-0.5 * gate * gate) / math.sqrt(2.0 * math.pi)
    return (gate * cumul, cumul + gate * density)


def contract_back(delta, weight):
    return lax.dot_general(
        delta, weight, (((1,), (1,)), ((), ())), preferred_element_type=jnp.float32
    )


def block_forward(residual_stream, weights, scale_gain, shift_bias):
    weight_in, weight_ffin, weight_ffout, weight_out = weights
    hidden = weight_ffout.shape[0]
    residual_reduced = residual_stream.astype(jnp.bfloat16)
    inner = jnp.dot(residual_reduced, weight_in, preferred_element_type=jnp.float32)
    centred_input = inner - jnp.mean(inner, axis=-1, keepdims=True)
    inverse_deviation = lax.rsqrt(
        jnp.mean(centred_input * centred_input, axis=-1, keepdims=True) + 1e-05
    )
    standardized_input = centred_input * inverse_deviation
    normalized_input = (standardized_input * scale_gain + shift_bias).astype(jnp.bfloat16)
    projected = jnp.dot(normalized_input, weight_ffin, preferred_element_type=jnp.float32)
    value_output = projected[:, :hidden]
    gate = projected[:, hidden:]
    gelu_result, gelu_derivative = gelu_parts(gate)
    mixed_hidden = (value_output * gelu_result).astype(jnp.bfloat16)
    inner_two = inner + jnp.dot(mixed_hidden, weight_ffout, preferred_element_type=jnp.float32)
    inner_reduced = inner_two.astype(jnp.bfloat16)
    residual_stream = residual_stream + jnp.dot(
        inner_reduced, weight_out, preferred_element_type=jnp.float32
    )
    return (
        residual_stream,
        (
            residual_reduced,
            standardized_input,
            inverse_deviation,
            normalized_input,
            value_output,
            gelu_result,
            gelu_derivative,
            mixed_hidden,
            inner_reduced,
        ),
    )


def block_backward(dstream, saved_activations, weights, scale_gain):
    weight_in, weight_ffin, weight_ffout, weight_out = weights
    (
        residual_reduced,
        standardized_input,
        inverse_deviation,
        normalized_input,
        value_output,
        gelu_result,
        gelu_derivative,
        mixed_hidden,
        inner_reduced,
    ) = saved_activations
    dout_low = dstream.astype(jnp.bfloat16)
    second_inner_gradient = contract_back(dout_low, weight_out)
    dtwo_low = second_inner_gradient.astype(jnp.bfloat16)
    dmixed = contract_back(dtwo_low, weight_ffout)
    dproj_low = jnp.concatenate(
        [dmixed * gelu_result, dmixed * value_output * gelu_derivative], axis=-1
    ).astype(jnp.bfloat16)
    dnormed = contract_back(dproj_low, weight_ffin)
    scaled_hidden = dnormed * scale_gain
    inner_gradient = second_inner_gradient + inverse_deviation * (
        scaled_hidden
        - jnp.mean(scaled_hidden, axis=-1, keepdims=True)
        - standardized_input * jnp.mean(scaled_hidden * standardized_input, axis=-1, keepdims=True)
    )
    dinner_low = inner_gradient.astype(jnp.bfloat16)
    dstream = dstream + contract_back(dinner_low, weight_in)
    records = [
        (residual_reduced, dinner_low),
        (normalized_input, dproj_low),
        (mixed_hidden, dtwo_low),
        (inner_reduced, dout_low),
    ]
    return (dstream, records)


def project_layer(inputs, deltas, sketch_in, sketch_out, samples):
    left = jnp.dot(inputs, sketch_in, preferred_element_type=jnp.float32)
    right = jnp.dot(deltas, sketch_out, preferred_element_type=jnp.float32)
    left = left.reshape(samples, -1, left.shape[-1])
    right = right.reshape(samples, -1, right.shape[-1])
    outer = jnp.einsum("srk,srj->skj", left, right, precision=lax.Precision.HIGHEST)
    return outer.reshape(samples, -1)


def sketches_of(block, sketch_cin, sketch_fin, sketch_cout, sketch_fout):
    return [
        (sketch_cin[block, 0], sketch_cout[block, 0]),
        (sketch_cin[block, 1], sketch_fout[block]),
        (sketch_fin[block], sketch_cout[block, 1]),
        (sketch_cin[block, 2], sketch_cout[block, 2]),
    ]


def on_device(
    clean_feats,
    noise_draw,
    timesteps,
    weight_in,
    weight_ffin,
    weight_ffout,
    weight_out,
    norm_gain,
    norm_bias,
    sketch_cin,
    sketch_fin,
    sketch_cout,
    sketch_fout,
    precond,
    store_grads,
    store_scale,
):
    samples = clean_feats.shape[0]
    positions = clean_feats.shape[2] * lax.axis_size("corpus")
    loss_scale = 1.0 / math.sqrt(clean_feats.shape[1] * positions)
    blocks = weight_in.shape[0]
    signal, spread = noise_levels(timesteps)
    noise_rows = noise_draw.astype(jnp.float32)
    residual_stream = (
        signal[:, :, None, None] * clean_feats.astype(jnp.float32)
        + spread[:, :, None, None] * noise_rows
    )
    residual_stream = residual_stream.reshape(-1, residual_stream.shape[-1])
    noise_rows = noise_rows.reshape(-1, noise_rows.shape[-1])
    gathered = (
        lax.all_gather(weight_in, "corpus", axis=2, tiled=True),
        lax.all_gather(weight_ffin, "corpus", axis=2, tiled=True),
        lax.all_gather(weight_ffout, "corpus", axis=2, tiled=True),
        lax.all_gather(weight_out, "corpus", axis=2, tiled=True),
    )

    def fetch_forward(block):
        return tuple((member[block] for member in gathered))

    def fetch_backward(block):
        return tuple((member[block] for member in gathered))

    saved_all = []
    for block in range(blocks):
        residual_stream, saved_activations = block_forward(
            residual_stream, fetch_forward(block), norm_gain[block], norm_bias[block]
        )
        saved_all.append(saved_activations)
    dstream = (residual_stream - noise_rows) * loss_scale
    layers = [None] * (4 * blocks)
    for block in reversed(range(blocks)):
        dstream, records = block_backward(
            dstream, saved_all[block], fetch_backward(block), norm_gain[block]
        )
        pairs = sketches_of(block, sketch_cin, sketch_fin, sketch_cout, sketch_fout)
        for index in range(4):
            layers[4 * block + index] = project_layer(
                records[index][0], records[index][1], pairs[index][0], pairs[index][1], samples
            )
    partial_grads = jnp.stack(layers, axis=1)
    totals = lax.psum(partial_grads, "corpus")
    routed = lax.all_to_all(totals, "query", split_axis=1, concat_axis=0, tiled=True)
    owned = jnp.einsum("qlk,lkj->qlj", routed, precond, precision=lax.Precision.HIGHEST).astype(
        jnp.bfloat16
    )
    preconditioned = lax.all_gather(owned, "query", axis=1, tiled=True)
    flat = preconditioned.reshape(preconditioned.shape[0], -1)
    raw = lax.dot_general(
        flat, store_grads, (((1,), (1,)), ((), ())), preferred_element_type=jnp.float32
    )
    return raw * store_scale[None, :]


def solution(mesh):
    placed = (
        P("query", None, "corpus", None),
        P("query", None, "corpus", None),
        P("query", None),
        P(None, None, "corpus"),
        P(None, None, "corpus"),
        P(None, None, "corpus"),
        P(None, None, "corpus"),
        P(),
        P(),
        P(),
        P(),
        P(),
        P(),
        P("query", None, None),
        P(("query", "corpus"), None),
        P(("query", "corpus")),
    )
    return jax.shard_map(
        on_device,
        mesh=mesh,
        in_specs=placed,
        out_specs=P(None, ("query", "corpus")),
        check_vma=False,
    )
```

profile of v0, /device:TPU:0, one launch (start us, length us, event | category | flops | bytes accessed | tf_op | source)
XLA Modules:
  0.0 167.8 jit_solution(465755251760985908)
XLA Ops:
  6.5 0.7 all-gather.5.cloned.1.call-update
  7.3 0.7 all-gather.3.cloned.1.call-update
  8.0 25.0 %all_gather.15 = bf16[2,320,320]{1,0,2:T(2,128)(2,1)S(1)} all-gather(bf16[2,320,20]{1,0,2:T(2,128)(2,1)} %param.19), channel_id=1, replica_groups=mesh['query'=2,'corpus'=16] {'corpus'}, dimensions={2}, use_global_device_ids=true | all-gather | bytes 435200 | tf_op jit(solution)/shard_map/all_gather | solution.py:155
  33.0 0.7 fusion.105
  33.7 0.9 copy.52
  34.6 19.7 %all_gather.18 = bf16[2,320,320]{1,0,2:T(2,128)(2,1)S(1)} all-gather(bf16[2,320,20]{1,0,2:T(2,128)(2,1)S(1)} %copy-done.12), channel_id=1, replica_groups=mesh['query'=2,'corpus'=16] {'corpus'}, dimensions={2}, use_global_device_ids=true | all-gather | bytes 435200 | tf_op jit(solution)/shard_map/all_gather | solution.py:158
  54.3 0.7 fusion.104
  55.0 0.9 copy.54
  55.9 0.9 copy.55
  56.8 0.9 copy.57
  57.7 0.6 slice_reduce_fusion
  58.6 0.7 fusion.102
  59.3 0.3 fusion.106
  59.8 0.8 fusion.79
  60.7 0.6 copy-done.4
  61.3 0.8 fusion.76
  62.2 5.7 %fusion.103 = (bf16[1,1280,320]{1,0,2:T(2,128)(2,1)}, bf16[1,1280,320]{1,0,2:T(2,128)(2,1)S(1)}) fusion(bf16[2,1280,320]{1,0,2:T(2,128)(2,1)} %all-gather.5.cloned.1.call-done), kind=kLoop, calls=%fused_computation.161 | loop fusion | bytes 3276800 | tf_op jit(solution)/shard_map/slice | solution.py:162
  67.9 36.5 %all-gather.3.cloned.1.call-done = bf16[2,320,2560]{1,2,0:T(8,128)(2,1)} async-done(((bf16[2,320,160]{1,2,0:T(8,128)(2,1)}), bf16[2,320,2560]{1,2,0:T(8,128)(2,1)}) %all-gather.3.cloned.1.call-update) | async-done | bytes 3276816 | tf_op jit(solution)/shard_map/all_gather | solution.py:156
  104.3 2.5 %fusion.1 = f32[64,2560]{1,0:T(8,128)S(1)} fusion(bf16[64,320]{1,0:T(8,128)(2,1)} %copy-done.4, bf16[2,320,2560]{1,2,0:T(8,128)(2,1)} %all-gather.3.cloned.1.call-done), kind=kOutput, calls=%fused_computation.3 | convolution fusion | flops 104857600 | bytes 2670592 | tf_op jit(solution)/shard_map/dot_general | solution.py:42
  106.9 0.4 fusion.8
  108.2 0.7 fusion.3
  109.0 0.3 copy-done.2
  109.3 0.4 fusion.9
  110.1 0.3 multiply_convert_fusion.1
  110.4 0.5 fusion.101
  111.5 0.3 multiply_convert_fusion
  113.7 0.5 fusion.100
  116.3 32.2 %psum.7 = f32[1,8,256]{2,0,1:T(1,128)S(1)} all-reduce(f32[1,8,256]{2,0,1:T(1,128)S(1)} %constant_dynamic-update-slice_fusion), channel_id=1, replica_groups=mesh['query'=2,'corpus'=16] {'corpus'}, use_global_device_ids=true, to_apply=%region_9.10 | all-reduce | flops 2048 | bytes 16384 | tf_op jit(solution)/shard_map/psum | solution.py:185
  148.6 6.3 %all_to_all.12 = f32[1,8,256]{2,0,1:T(1,128)S(1)} all-to-all(f32[1,8,256]{2,0,1:T(1,128)S(1)} %psum.7), channel_id=1, replica_groups=mesh['query'=2,'corpus'=16] {'query'}, dimensions={1} | all-to-all | bytes 16384 | tf_op jit(solution)/shard_map/all_to_all | solution.py:186
  155.0 0.6 fusion.11
  155.6 4.3 %all_gather.19 = bf16[2,8,256]{2,0,1:T(2,128)(2,1)S(1)} all-gather(bf16[2,4,256]{2,0,1:T(2,128)(2,1)S(1)} %fusion.11), channel_id=1, replica_groups=mesh['query'=2,'corpus'=16] {'query'}, dimensions={1}, use_global_device_ids=true | all-gather | bytes 12288 | tf_op jit(solution)/shard_map/all_gather | solution.py:190
  160.0 1.0 convolution_multiply_fusion
  (111 shorter events, 6.5 us)
Async XLA Ops:
  6.5 148.5 %copy-start = (f32[4,256,256]{2,1,0:T(8,128)S(1)}, f32[4,256,256]{2,1,0:T(8,128)}, u32[]{:S(2)}) copy-start(f32[4,256,256]{2,1,0:T(8,128)} %param.29) | copy-start | bytes 3145732
  6.5 28.1 %copy-start.12 = (bf16[2,320,20]{1,0,2:T(2,128)(2,1)S(1)}, bf16[2,320,20]{1,0,2:T(2,128)(2,1)}, u32[]{:S(2)}) copy-start(bf16[2,320,20]{1,0,2:T(2,128)(2,1)} %param.22) | copy-start | bytes 76804
  6.5 55.6 %all-gather.5.cloned.1.call-start = ((), (), s32[]{:S(2)}) async-start(), calls=%async_computation.2 | async-start | bytes 1740800 | tf_op jit(solution)/shard_map/all_gather | solution.py:157
  7.3 97.1 %all-gather.3.cloned.1.call-start = ((), (), s32[]{:S(2)}) async-start(), calls=%async_computation.1 | async-start | bytes 4177920 | tf_op jit(solution)/shard_map/all_gather | solution.py:156
  54.3 3.4 %copy-start.16 = (f32[2,320]{1,0:T(2,128)S(1)}, f32[2,320]{1,0:T(2,128)}, u32[]{:S(2)}) copy-start(f32[2,320]{1,0:T(2,128)} %param.24) | copy-start | bytes 7684
  54.3 4.0 %copy-start.17 = (f32[2,320]{1,0:T(2,128)S(1)}, f32[2,320]{1,0:T(2,128)}, u32[]{:S(2)}) copy-start(f32[2,320]{1,0:T(2,128)} %param.23) | copy-start | bytes 7684
  54.3 4.0 %copy-start.21 = (s32[1,2]{1,0:T(1,128)S(1)}, s32[1,2]{1,0:T(1,128)}, u32[]{:S(2)}) copy-start(s32[1,2]{1,0:T(1,128)} %param.18) | copy-start | bytes 28
  54.3 4.3 %copy-start.6 = (bf16[1,2,32,320]{3,2,1,0:T(8,128)(2,1)S(1)}, bf16[1,2,32,320]{3,2,1,0:T(8,128)(2,1)}, u32[]{:S(2)}) copy-start(bf16[1,2,32,320]{3,2,1,0:T(8,128)(2,1)} %param.17) | copy-start | bytes 122884
  54.3 4.3 %copy-start.11 = (bf16[1,2,32,320]{3,2,1,0:T(8,128)(2,1)S(1)}, bf16[1,2,32,320]{3,2,1,0:T(8,128)(2,1)}, u32[]{:S(2)}) copy-start(bf16[1,2,32,320]{3,2,1,0:T(8,128)(2,1)} %param.16) | copy-start | bytes 122884
  59.6 8.3 %copy-start.14 = (f32[64]{0:T(128)}, f32[64]{0:T(128)S(1)}, u32[]{:S(2)}) copy-start(f32[64]{0:T(128)S(1)} %broadcast_multiply_fusion.5) | copy-start | bytes 772
  59.8 2.4 %copy-start.18 = (f32[64]{0:T(128)}, f32[64]{0:T(128)S(1)}, u32[]{:S(2)}) copy-start(f32[64]{0:T(128)S(1)} %add_rsqrt_fusion.1) | copy-start | bytes 772
  60.7 0.6 copy-start.4
  104.3 2.9 %copy-start.10 = (bf16[2,3,320,16]{2,3,1,0:T(8,128)(2,1)S(1)}, bf16[2,3,320,16]{2,3,1,0:T(8,128)(2,1)}, u32[]{:S(2)}) copy-start(bf16[2,3,320,16]{2,3,1,0:T(8,128)(2,1)} %param.25) | copy-start | bytes 184324
  104.3 3.1 %copy-start.5 = (f32[1,2,32,320]{3,2,1,0:T(8,128)S(1)}, f32[1,2,32,320]{3,2,1,0:T(8,128)}, u32[]{:S(2)}) copy-start(f32[1,2,32,320]{3,2,1,0:T(8,128)} %get-tuple-element.14) | copy-start | bytes 245764
  104.3 3.9 %copy-start.1 = (bf16[2,320,2560]{1,2,0:T(8,128)(2,1)S(1)}, bf16[2,320,2560]{1,2,0:T(8,128)(2,1)}, u32[]{:S(2)}) copy-start(bf16[2,320,2560]{1,2,0:T(8,128)(2,1)} %all-gather.3.cloned.1.call-done) | copy-start | bytes 9830404
  106.8 1.3 copy-start.13
  107.9 1.4 copy-start.2
  108.2 1.5 copy-start.7
  110.9 0.9 copy-start.9
  110.9 1.6 copy-start.8
  111.3 2.0 %copy-start.22 = (bf16[2,2560,16]{1,2,0:T(8,128)(2,1)S(1)}, bf16[2,2560,16]{1,2,0:T(8,128)(2,1)}, u32[]{:S(2)}) copy-start(bf16[2,2560,16]{1,2,0:T(8,128)(2,1)} %param.28) | copy-start | bytes 491524
  111.5 2.2 %copy-start.15 = (f32[64]{0:T(128)S(1)}, f32[64]{0:T(128)}, u32[]{:S(2)}) copy-start(f32[64]{0:T(128)} %copy-done.14) | copy-start | bytes 772
  111.5 2.2 %copy-start.19 = (f32[64]{0:T(128)S(1)}, f32[64]{0:T(128)}, u32[]{:S(2)}) copy-start(f32[64]{0:T(128)} %copy-done.18) | copy-start | bytes 772
  113.7 46.3 %copy-start.3 = (bf16[256,2048]{1,0:T(8,128)(2,1)S(1)}, bf16[256,2048]{1,0:T(8,128)(2,1)}, u32[]{:S(2)}) copy-start(bf16[256,2048]{1,0:T(8,128)(2,1)} %param.30) | copy-start | bytes 3145732
  113.7 46.3 %copy-start.20 = (f32[256]{0:T(256)S(1)}, f32[256]{0:T(256)}, u32[]{:S(2)}) copy-start(f32[256]{0:T(256)} %param.31) | copy-start | bytes 3076
Sparse Core Ops, SparseCore 0:
  9.5 43.8 all-gather.4
  55.7 48.5 all-gather.2
where the time goes:
time: 168 us
  blocking collectives  87.6 us (52%)
  waiting for transfers between devices  37.9 us (23%)
  between operations  13.9 us (8%)
  matrix products  13.5 us (8%)
  local copies, waits for them, and re-layouts  13 us (8%)
  other arithmetic  1.84 us (1%)
    all_gather x1, waiting for transfers between devices, on_device(): lax.all_gather(weight_ffin, 'corpus', axis=2, tiled=True)  36.5 us
    psum x1, blocking collectives, on_device(): totals = lax.psum(partial_grads, 'corpus')  32.2 us
    all_gather x1, blocking collectives, on_device(): lax.all_gather(weight_in, 'corpus', axis=2, tiled=True)  25 us
    all_gather x1, blocking collectives, on_device(): lax.all_gather(weight_out, 'corpus', axis=2, tiled=True)  19.7 us
    slice x3, local copies, waits for them, and re-layouts, fetch_forward(): return tuple((member[block] for member in gathered))  7.04 us
    all_to_all x1, blocking collectives, on_device(): lax.all_to_all(totals, 'query', split_axis=1, concat_axis=0, tiled=True)  6.35 us
    unnamed x57, local copies, waits for them, and re-layouts  4.61 us
    all_gather x1, blocking collectives, on_device(): preconditioned = lax.all_gather(owned, 'query', axis=1, tiled=True)  4.33 us
  transfers between devices with their start and end apart: 2, of which 1 were waited for; matrix products, arithmetic and copies ran while one was open for 9% of the time, Pallas kernels for 0%

commit v1 on v0

--- a/solution.py
+++ b/solution.py
@@ -139,6 +139,20 @@
     store_grads,
     store_scale,
 ):
+
+    def boxes_deliver(row_data):
+        chip_axis = "corpus"
+        spare = lax.psum(1, chip_axis)
+        u1, prior = (spare, lax.axis_index(chip_axis))
+        v_next, built = (row_data, 1)
+        while built < u1:
+            z1 = lax.ppermute(v_next, chip_axis, list(map(lambda i: (i, i ^ built), range(u1))))
+            now = jnp.concatenate([v_next, z1], axis=2)
+            x_new = jnp.concatenate([z1, v_next], 2)
+            v_next = jnp.where(prior & built == 0, now, x_new)
+            built = 2 * built
+        return v_next
+
     samples = clean_feats.shape[0]
     positions = clean_feats.shape[2] * lax.axis_size("corpus")
     loss_scale = 1.0 / math.sqrt(clean_feats.shape[1] * positions)
@@ -153,7 +167,7 @@
     noise_rows = noise_rows.reshape(-1, noise_rows.shape[-1])
     gathered = (
         lax.all_gather(weight_in, "corpus", axis=2, tiled=True),
-        lax.all_gather(weight_ffin, "corpus", axis=2, tiled=True),
+        boxes_deliver(weight_ffin),
         lax.all_gather(weight_ffout, "corpus", axis=2, tiled=True),
         lax.all_gather(weight_out, "corpus", axis=2, tiled=True),
     )

time: 168 us -> 229 us (1.36)
  waiting for transfers between devices: 37.9 us -> 62.3 us
  blocking collectives: 87.6 us -> 109 us
  other arithmetic: 1.84 us -> 7.9 us
  local copies, waits for them, and re-layouts: 13 us -> 18.7 us
  starting transfers between devices: 0.04 us -> 3.62 us
    ppermute x0 -> x4, waiting for transfers between devices: none -> 62.3 us  [boxes_deliver(): lax.ppermute(v_next, chip_axis, list(map(lambda i: (i, i ^ built), range(...]
    all_gather x1 -> x0, waiting for transfers between devices: 36.5 us -> none  [on_device(): lax.all_gather(weight_ffin, 'corpus', axis=2, tiled=True)]
    all_gather x1, blocking collectives: 19.7 us -> 37.9 us  [on_device(): lax.all_gather(weight_out, 'corpus', axis=2, tiled=True)]
    select_n x0 -> x4, other arithmetic: none -> 5.39 us  [boxes_deliver(): v_next = jnp.where(prior & built == 0, now, x_new)]
    all_gather x1, blocking collectives: 25 us -> 30.4 us  [on_device(): lax.all_gather(weight_in, 'corpus', axis=2, tiled=True)]
    unnamed x57 -> x60, local copies, waits for them, and re-layouts: 4.61 us -> 9.49 us
    ppermute x0 -> x4, starting transfers between devices: none -> 3.62 us  [boxes_deliver(): lax.ppermute(v_next, chip_axis, list(map(lambda i: (i, i ^ built), range(...]
    dot_general x2, matrix products: 3.18 us -> 0.87 us  [block_forward(): jnp.dot(normalized_input, weight_ffin, preferred_element_type=jnp.float32)]
  transfers between devices with their start and end apart: 2 -> 5, of which waited for: 1 -> 2; matrix products, arithmetic and copies ran while one was open for 9% -> 9% of each run, Pallas kernels for 0% -> 0%
where the time goes in v1:
time: 229 us
  blocking collectives  109 us (48%)
  waiting for transfers between devices  62.3 us (27%)
  local copies, waits for them, and re-layouts  18.7 us (8%)
  between operations  13.9 us (6%)
  matrix products  13.3 us (6%)
  other arithmetic  7.9 us (3%)
  starting transfers between devices  3.62 us (2%)
    ppermute x4, waiting for transfers between devices, boxes_deliver(): lax.ppermute(v_next, chip_axis, list(map(lambda i: (i, i ^ built), range(...  62.3 us
    all_gather x1, blocking collectives, on_device(): lax.all_gather(weight_out, 'corpus', axis=2, tiled=True)  37.9 us
    all_gather x1, blocking collectives, on_device(): lax.all_gather(weight_in, 'corpus', axis=2, tiled=True)  30.4 us
    psum x1, blocking collectives, on_device(): totals = lax.psum(partial_grads, 'corpus')  30.2 us
    unnamed x60, local copies, waits for them, and re-layouts  9.49 us
    slice x3, local copies, waits for them, and re-layouts, fetch_forward(): return tuple((member[block] for member in gathered))  7.84 us
    all_to_all x1, blocking collectives, on_device(): lax.all_to_all(totals, 'query', split_axis=1, concat_axis=0, tiled=True)  6.35 us
    select_n x4, other arithmetic, boxes_deliver(): v_next = jnp.where(prior & built == 0, now, x_new)  5.39 us
  transfers between devices with their start and end apart: 5, of which 2 were waited for; matrix products, arithmetic and copies ran while one was open for 9% of the time, Pallas kernels for 0%

profile of v1, /device:TPU:0, one launch (start us, length us, event | category | flops | bytes accessed | tf_op | source)
XLA Modules:
  0.0 228.9 jit_solution(3959445959421087402)
XLA Ops:
  6.5 1.2 copy.41
  7.8 0.5 collective-permute-start
  8.3 0.8 fusion.93
  10.0 3.0 %collective-permute-start.1 = (bf16[2,320,320]{2,1,0:T(8,128)(2,1)S(1)}, bf16[2,320,320]{2,1,0:T(8,128)(2,1)S(1)}, u32[]{:S(2)}, u32[]{:S(2)}) collective-permute-start(bf16[2,320,320]{2,1,0:T(8,128)(2,1)S(1)} %maximum_select_fusion.3), channel_id=1, source_target_pairs={{0,2},{1,3},{2,0},{3,1},{4,6},{5,7},{6,4},{7,5},{8,10},{9,11},{10,... | collective-permute-start | bytes 1228808 | tf_op jit(solution)/shard_map/ppermute | solution.py:149
  12.9 30.4 %all_gather.12 = bf16[2,320,320]{1,0,2:T(2,128)(2,1)S(1)} all-gather(bf16[2,320,20]{1,0,2:T(2,128)(2,1)S(1)} %copy-done.13), channel_id=1, replica_groups=mesh['query'=2,'corpus'=16] {'corpus'}, dimensions={2}, use_global_device_ids=true | all-gather | bytes 435200 | tf_op jit(solution)/shard_map/all_gather | solution.py:169
  43.3 0.6 maximum_select_fusion.2
  44.0 37.9 %all_gather.14 = bf16[2,320,320]{1,0,2:T(2,128)(2,1)S(1)} all-gather(bf16[2,320,20]{1,0,2:T(2,128)(2,1)S(1)} %copy-done.14), channel_id=1, replica_groups=mesh['query'=2,'corpus'=16] {'corpus'}, dimensions={2}, use_global_device_ids=true | all-gather | bytes 435200 | tf_op jit(solution)/shard_map/all_gather | solution.py:172
  81.9 0.8 fusion.102
  82.6 1.6 fusion.105
  84.3 1.7 fusion.104
  85.9 1.8 maximum_select_fusion.1
  87.8 2.0 copy.58
  89.8 1.5 copy.60
  91.3 1.5 copy.61
  92.8 1.5 copy.63
  94.3 0.6 slice_reduce_fusion.1
  94.9 1.2 fusion.106
  96.4 0.9 fusion.79
  97.4 0.8 fusion.76
  98.2 61.9 %collective-permute-done.3 = bf16[2,320,1280]{2,1,0:T(8,128)(2,1)} collective-permute-done((bf16[2,320,1280]{2,1,0:T(8,128)(2,1)S(1)}, bf16[2,320,1280]{2,1,0:T(8,128)(2,1)}, u32[]{:S(2)}, u32[]{:S(2)}) %collective-permute-start.3) | collective-permute-done | bytes 1638432 | tf_op jit(solution)/shard_map/ppermute | solution.py:149
  160.2 2.6 %maximum_select_fusion = bf16[2,320,2560]{2,1,0:T(8,128)(2,1)S(1)} fusion(bf16[2,320,1280]{2,1,0:T(8,128)(2,1)} %collective-permute-done.3, bf16[2,320,1280]{2,1,0:T(8,128)(2,1)S(1)} %maximum_select_fusion.1, pred[]{:T(512)S(6)} %eq.12), kind=kLoop, calls=%fused_computation | loop fusion | flops 14745600 | bytes 6553601 | tf_op jit(solution)/shard_map/jit(_where)/select_n | solution.py:152
  162.8 1.7 copy-done.1
  164.5 0.4 fusion.1
  165.1 4.5 %fusion.103 = (bf16[1,1280,320]{1,0,2:T(2,128)(2,1)S(1)}, bf16[1,1280,320]{1,0,2:T(2,128)(2,1)S(1)}) fusion(bf16[2,1280,320]{1,0,2:T(2,128)(2,1)} %all-gather.2.cloned.1.call-done), kind=kLoop, calls=%fused_computation.165 | loop fusion | bytes 3276800 | tf_op jit(solution)/shard_map/slice | solution.py:176
  172.6 0.7 fusion.101
  174.9 0.7 fusion.100
  176.4 0.8 fusion.63
  179.5 30.2 %psum.7 = f32[1,8,256]{2,0,1:T(1,128)S(1)} all-reduce(f32[1,8,256]{2,0,1:T(1,128)S(1)} %constant_dynamic-update-slice_fusion), channel_id=1, replica_groups=mesh['query'=2,'corpus'=16] {'corpus'}, use_global_device_ids=true, to_apply=%region_9.10 | all-reduce | flops 2048 | bytes 16384 | tf_op jit(solution)/shard_map/psum | solution.py:199
  209.8 6.4 %all_to_all.12 = f32[1,8,256]{2,0,1:T(1,128)S(1)} all-to-all(f32[1,8,256]{2,0,1:T(1,128)S(1)} %psum.7), channel_id=1, replica_groups=mesh['query'=2,'corpus'=16] {'query'}, dimensions={1} | all-to-all | bytes 16384 | tf_op jit(solution)/shard_map/all_to_all | solution.py:200
  216.2 0.6 fusion.11
  216.8 4.3 %all_gather.15 = bf16[2,8,256]{2,0,1:T(2,128)(2,1)S(1)} all-gather(bf16[2,4,256]{2,0,1:T(2,128)(2,1)S(1)} %fusion.11), channel_id=1, replica_groups=mesh['query'=2,'corpus'=16] {'query'}, dimensions={1}, use_global_device_ids=true | all-gather | bytes 12288 | tf_op jit(solution)/shard_map/all_gather | solution.py:204
  221.1 1.0 convolution_multiply_fusion
  (123 shorter events, 8.9 us)
Async XLA Ops:
  6.5 209.6 %copy-start = (f32[4,256,256]{2,1,0:T(8,128)S(1)}, f32[4,256,256]{2,1,0:T(8,128)}, u32[]{:S(2)}) copy-start(f32[4,256,256]{2,1,0:T(8,128)} %param.29) | copy-start | bytes 3145732
  6.5 6.4 %copy-start.13 = (bf16[2,320,20]{1,0,2:T(2,128)(2,1)S(1)}, bf16[2,320,20]{1,0,2:T(2,128)(2,1)}, u32[]{:S(2)}) copy-start(bf16[2,320,20]{1,0,2:T(2,128)(2,1)} %param.19) | copy-start | bytes 76804
  6.5 158.5 %all-gather.2.cloned.1.call-start = ((), (), s32[]{:S(2)}) async-start(), calls=%async_computation.1 | async-start | bytes 1740800 | tf_op jit(solution)/shard_map/all_gather | solution.py:171
  7.8 1.8 collective-permute-start
  9.2 34.8 %copy-start.14 = (bf16[2,320,20]{1,0,2:T(2,128)(2,1)S(1)}, bf16[2,320,20]{1,0,2:T(2,128)(2,1)}, u32[]{:S(2)}) copy-start(bf16[2,320,20]{1,0,2:T(2,128)(2,1)} %param.22) | copy-start | bytes 76804
  9.9 71.9 %copy-start.7 = (bf16[1,2,32,320]{3,2,1,0:T(8,128)(2,1)S(1)}, bf16[1,2,32,320]{3,2,1,0:T(8,128)(2,1)}, u32[]{:S(2)}) copy-start(bf16[1,2,32,320]{3,2,1,0:T(8,128)(2,1)} %param.17) | copy-start | bytes 122884
  10.0 71.9 %copy-start.12 = (bf16[1,2,32,320]{3,2,1,0:T(8,128)(2,1)S(1)}, bf16[1,2,32,320]{3,2,1,0:T(8,128)(2,1)}, u32[]{:S(2)}) copy-start(bf16[1,2,32,320]{3,2,1,0:T(8,128)(2,1)} %param.16) | copy-start | bytes 122884
  10.0 33.3 %collective-permute-start.1 = (bf16[2,320,320]{2,1,0:T(8,128)(2,1)S(1)}, bf16[2,320,320]{2,1,0:T(8,128)(2,1)S(1)}, u32[]{:S(2)}, u32[]{:S(2)}) collective-permute-start(bf16[2,320,320]{2,1,0:T(8,128)(2,1)S(1)} %maximum_select_fusion.3), channel_id=1, source_target_pairs={{0,2},{1,3},{2,0},{3,1},{4,6},{5,7},{6,4},{7,5},{8,10},{9,11},{10,... | collective-permute-start | bytes 1228808 | tf_op jit(solution)/shard_map/ppermute | solution.py:149
  43.9 42.0 %collective-permute-start.2 = (bf16[2,320,640]{2,1,0:T(8,128)(2,1)S(1)}, bf16[2,320,640]{2,1,0:T(8,128)(2,1)}, u32[]{:S(2)}, u32[]{:S(2)}) collective-permute-start(bf16[2,320,640]{2,1,0:T(8,128)(2,1)S(1)} %maximum_select_fusion.2), channel_id=1, source_target_pairs={{0,4},{1,5},{2,6},{3,7},{4,0},{5,1},{6,2},{7,3},{8,12},{9,13},{10,... | collective-permute-start | bytes 2457608 | tf_op jit(solution)/shard_map/ppermute | solution.py:149
  85.9 1.9 copy-start.18
  87.7 6.6 %copy-start.19 = (f32[2,320]{1,0:T(2,128)S(1)}, f32[2,320]{1,0:T(2,128)}, u32[]{:S(2)}) copy-start(f32[2,320]{1,0:T(2,128)} %param.23) | copy-start | bytes 7684
  87.7 72.4 %collective-permute-start.3 = (bf16[2,320,1280]{2,1,0:T(8,128)(2,1)S(1)}, bf16[2,320,1280]{2,1,0:T(8,128)(2,1)}, u32[]{:S(2)}, u32[]{:S(2)}) collective-permute-start(bf16[2,320,1280]{2,1,0:T(8,128)(2,1)S(1)} %maximum_select_fusion.1), channel_id=1, source_target_pairs={{0,8},{1,9},{2,10},{3,11},{4,12},{5,13},{6,14},{7,15},{8,0},{9,1},... | collective-permute-start | bytes 4915208 | tf_op jit(solution)/shard_map/ppermute | solution.py:149
  96.1 1.1 copy-start.16
  96.3 66.5 %copy-start.20 = (f32[64]{0:T(128)}, f32[64]{0:T(128)S(1)}, u32[]{:S(2)}) copy-start(f32[64]{0:T(128)S(1)} %add_rsqrt_fusion.1) | copy-start | bytes 772
  162.8 1.7 copy-start.1
  165.0 4.6 %copy-start.4 = (bf16[64,1280]{1,0:T(8,128)(2,1)}, bf16[64,1280]{1,0:T(8,128)(2,1)S(1)}, u32[]{:S(2)}) copy-start(bf16[64,1280]{1,0:T(8,128)(2,1)S(1)} %multiply_convert_fusion.3) | copy-start | bytes 491524
  165.0 5.0 %copy-start.11 = (bf16[2,3,320,16]{2,3,1,0:T(8,128)(2,1)S(1)}, bf16[2,3,320,16]{2,3,1,0:T(8,128)(2,1)}, u32[]{:S(2)}) copy-start(bf16[2,3,320,16]{2,3,1,0:T(8,128)(2,1)} %param.25) | copy-start | bytes 184324
  165.0 5.1 %copy-start.6 = (f32[1,2,32,320]{3,2,1,0:T(8,128)S(1)}, f32[1,2,32,320]{3,2,1,0:T(8,128)}, u32[]{:S(2)}) copy-start(f32[1,2,32,320]{3,2,1,0:T(8,128)} %get-tuple-element.14) | copy-start | bytes 245764
  165.1 5.9 %copy-start.2 = (bf16[2,320,2560]{2,1,0:T(8,128)(2,1)S(1)}, bf16[2,320,2560]{2,1,0:T(8,128)(2,1)}, u32[]{:S(2)}) copy-start(bf16[2,320,2560]{2,1,0:T(8,128)(2,1)} %copy-done.1) | copy-start | bytes 9830404
  169.6 1.2 copy-start.15
  170.9 0.9 copy-start.8
  173.3 0.9 copy-start.10
  173.4 1.4 copy-start.17
  173.4 1.4 copy-start.21
  174.2 1.4 copy-start.23
  174.8 1.1 copy-start.5
  174.8 1.1 copy-start.9
  175.8 45.3 %copy-start.3 = (bf16[256,2048]{1,0:T(8,128)(2,1)S(1)}, bf16[256,2048]{1,0:T(8,128)(2,1)}, u32[]{:S(2)}) copy-start(bf16[256,2048]{1,0:T(8,128)(2,1)} %param.30) | copy-start | bytes 3145732
  175.8 45.3 %copy-start.22 = (f32[256]{0:T(256)S(1)}, f32[256]{0:T(256)}, u32[]{:S(2)}) copy-start(f32[256]{0:T(256)} %param.31) | copy-start | bytes 3076
Sparse Core Ops, SparseCore 0:
  9.5 44.6 all-gather.1
